TPU v7x, 32 devices: a whole 2x2x4 slice. The times are simulated.
32 devices in a mesh: row: 4 (over x, core), loop: 8 (over z, y).
Axes of the slice: x: 2, y: 2, z: 4, core: 2. Of those that a mesh axis runs over, the one named last changes fastest.
Arguments:
- amplitudes: float32 [8192, 6144], P('row', 'loop'), may hold values from -6 to 6
- integrals: float32 [8192, 2048], P('row', 'loop'), may hold values from -0.09375 to 0.09375
- screen_mask: int32 [64, 16], P('row'), may hold values 0 or 1
- base_residual: float32 [2048, 6144], P('row', 'loop'), may hold values from -6 to 6
- vir_energy: float32 [2048], P('row'), may hold values from 0.5 to 4
- occ_energy: float32 [6144], P('loop'), may hold values from 0.5 to 2
Outputs:
- residual: float32 [2048, 6144], P('row', 'loop')
- update: float32 [2048, 6144], P('row', 'loop')
All inputs are finite; a program needn't handle non-finite values. No bound on the sum of `screen_mask` on one device may be relied on, other than what follows from the above.
Results may differ from a plain program's by a relative error of at most 0.000068.
Values sent between devices are 32-bit elements; how exact they have to be, the bound alone decides.
No kernel may reach another device: no remote copies, remote signals or barrier semaphores. Data moves between devices by JAX's collectives and lax.ppermute only.
A program may use at most 128 MiB of HBM per device.

v0:
```python
import jax
import jax.numpy as jnp
from jax import lax
from jax.sharding import PartitionSpec as P

TILE = 128


def expand_mask(screen_mask, tile):
    rows_t, cols_t = screen_mask.shape
    values = screen_mask.astype(jnp.float32)
    return jnp.broadcast_to(values[:, None, :, None], (rows_t, tile, cols_t, tile)).reshape(
        rows_t * tile, cols_t * tile
    )


def contract(panel, amplitudes):
    return lax.dot_general(
        panel,
        amplitudes,
        (((0,), (0,)), ((), ())),
        precision=lax.Precision.HIGHEST,
        preferred_element_type=jnp.float32,
    )


def on_device(amplitudes, integrals, screen_mask, base_residual, vir_energy, occ_energy):
    full_mask = expand_mask(screen_mask, TILE)
    assembled = lax.all_gather(integrals, "loop", axis=1, tiled=True)
    screened = assembled * full_mask
    ladder = lax.psum_scatter(
        contract(screened, amplitudes), "row", scatter_dimension=0, tiled=True
    )
    residual = base_residual + ladder
    update = residual / (vir_energy[:, None] + occ_energy[None, :])
    return (residual, update)


def solution(mesh):
    in_specs = (
        P("row", "loop"),
        P("row", "loop"),
        P("row", None),
        P("row", "loop"),
        P("row"),
        P("loop"),
    )
    out_specs = (P("row", "loop"), P("row", "loop"))
    return jax.shard_map(
        on_device, mesh=mesh, in_specs=in_specs, out_specs=out_specs, check_vma=False
    )
```

profile of v0, /device:TPU:10, one launch (start us, length us, event | category | flops | bytes accessed | tf_op | source)
XLA Modules:
  0.0 360.2 jit_solution(17750955621435998766)
XLA Ops:
  7.2 0.0 all-gather.2.cloned.1.call-start
  7.2 0.7 all-gather.2.cloned.1.call-update
  7.9 0.0 reduce-scatter.2.cloned.1.call-start
  7.9 0.7 convert_element_type.3
  8.6 228.5 %all-gather.2.cloned.1.call-done = f32[2048,2048]{1,0:T(8,128)} async-done(((f32[2048,256]{1,0:T(8,128)}), f32[2048,2048]{1,0:T(8,128)}) %all-gather.2.cloned.1.call-update) | async-done | bytes 16777232 | tf_op jit(solution)/shard_map/all_gather | solution.py:29
  237.1 1.1 broadcast_in_dim.2
  238.3 54.0 %fusion = f32[2048,768]{1,0:T(8,128)} fusion(f32[2048,768]{1,0:T(8,128)} %param.6, f32[2048,2048]{1,0:T(8,128)} %all-gather.2.cloned.1.call-done, f32[256,8,16,128]{3,2,1,0:T(8,128)S(1)} %bitcast.6), kind=kOutput, calls=%fused_computation.1 | convolution fusion | flops 38658899968 | bytes 46137344 | tf_op jit(solution)/shard_map/dot_general | solution.py:18
  292.3 0.0 copy-start
  292.3 0.0 copy-start.1
  292.3 0.0 copy-start.2
  292.3 0.0 reduce-scatter.2.cloned.1.call-update
  292.3 57.6 %reduce-scatter.2.cloned.1.call-done = f32[512,768]{1,0:T(8,128)} async-done(((f32[2048,768]{1,0:T(8,128)}), f32[512,768]{1,0:T(8,128)}) %reduce-scatter.2.cloned.1.call-update) | async-done | bytes 1572880 | tf_op jit(solution)/shard_map/reduce_scatter | solution.py:31
  350.0 0.0 copy-done
  350.0 0.0 copy-done.1
  350.0 0.0 copy-done.2
  350.0 3.3 add_divide_fusion
Async XLA Ops:
  7.2 230.0 %all-gather.2.cloned.1.call-start = ((), (), s32[]{:S(2)}) async-start(), calls=%async_computation.1 | async-start | bytes 18874368 | tf_op jit(solution)/shard_map/all_gather | solution.py:29
  7.9 342.1 %reduce-scatter.2.cloned.1.call-start = ((), (), s32[]{:S(2)}) async-start(), calls=%async_computation.2 | async-start | bytes 7864320 | tf_op jit(solution)/shard_map/reduce_scatter | solution.py:31
  292.3 57.7 %copy-start = (f32[512,768]{1,0:T(8,128)S(1)}, f32[512,768]{1,0:T(8,128)}, u32[]{:S(2)}) copy-start(f32[512,768]{1,0:T(8,128)} %param.9) | copy-start | bytes 4718596
  292.3 57.7 %copy-start.1 = (f32[768]{0:T(1024)S(1)}, f32[768]{0:T(1024)}, u32[]{:S(2)}) copy-start(f32[768]{0:T(1024)} %param.11) | copy-start | bytes 9220
  292.3 57.7 %copy-start.2 = (f32[512]{0:T(512)S(1)}, f32[512]{0:T(512)}, u32[]{:S(2)}) copy-start(f32[512]{0:T(512)} %param.10) | copy-start | bytes 6148
Sparse Core Ops, SparseCore 0:
  10.0 227.0 all-gather.1
  292.5 57.4 reduce-scatter.1
where the time goes:
time: 363 us; the launch traced here: 360 us
  waiting for transfers between devices  287 us (79%)
  matrix products  54 us (15%)
  between operations  14 us (4%)
  other arithmetic  4.05 us (1%)
    all_gather x1, waiting for transfers between devices, on_device(): assembled = lax.all_gather(integrals, 'loop', axis=1, tiled=True)  228 us
    reduce_scatter x1, waiting for transfers between devices, on_device(): lax.psum_scatter(contract(screened, amplitudes), 'row', scatter_dimension...  57.6 us
    dot_general x1, matrix products, contract(): lax.dot_general(panel, amplitudes, (((0,), (0,)), ((), ())), precision=la...  54 us
  transfers between devices with their start and end apart: 2, of which 2 were waited for; matrix products, arithmetic and copies ran while one was open for 0% of the time, Pallas kernels for 0%

commit v1 on v0

v1 whole, which is shorter than its diff:
```python
import functools

import jax
import jax.numpy as jnp
from jax import lax
from jax.experimental import pallas as pl
from jax.experimental.pallas import tpu as pltpu
from jax.sharding import PartitionSpec as P

TILE = 128
GROUP = 8
HEAD = 16
VMEM_LIMIT = 16 * 1024 * 1024
UNIT = 4

COST = pl.CostEstimate(flops=1, bytes_accessed=1, transcendentals=0)
STAGE_COST = pl.CostEstimate(flops=40 * 1150 * 10**6, bytes_accessed=1, transcendentals=0)
ANY = pl.BlockSpec(memory_space=pl.ANY)
SMEM = pl.BlockSpec(memory_space=pltpu.SMEM)
VMEM = pl.BlockSpec(memory_space=pltpu.VMEM)
HBM = pl.BlockSpec(memory_space=pltpu.HBM)


def expand_mask(screen_mask, tile):
    rows_t, cols_t = screen_mask.shape
    values = screen_mask.astype(jnp.float32)
    return jnp.broadcast_to(values[:, None, :, None], (rows_t, tile, cols_t, tile)).reshape(
        rows_t * tile, cols_t * tile
    )


def gathered(amplitudes, integrals, screen_mask, base_residual, vir_energy, occ_energy):
    full_mask = expand_mask(screen_mask, TILE)
    assembled = lax.all_gather(integrals, "loop", axis=1, tiled=True)
    partial = lax.dot_general(
        assembled * full_mask,
        amplitudes,
        (((0,), (0,)), ((), ())),
        precision=lax.Precision.HIGHEST,
        preferred_element_type=jnp.float32,
    )
    ladder = lax.psum_scatter(partial, "row", scatter_dimension=0, tiled=True)
    residual = base_residual + ladder
    return residual, residual / (vir_energy[:, None] + occ_energy[None, :])


def kept_in_block(mask_ref, block):
    total = jnp.int32(0)
    for i in range(mask_ref.shape[0]):
        total = total + mask_ref[i, 2 * block] + mask_ref[i, 2 * block + 1]
    return total


def needs_kernel(mask_ref, out_ref):
    def step(pair, carry):
        more, units = carry
        rest = jnp.int32(0)
        for which in range(2):
            count = kept_in_block(mask_ref, 2 * pair + which)
            more = jnp.maximum(more, (count > HEAD + GROUP).astype(jnp.int32))
            rest = rest + jnp.maximum(count - HEAD, 0)
        units = jnp.maximum(units, (jnp.maximum(rest - GROUP, 0) + UNIT - 1) // UNIT)
        return more, units

    more, units = lax.fori_loop(0, mask_ref.shape[1] // 4, step, (jnp.int32(0), jnp.int32(0)))
    row = lax.broadcasted_iota(jnp.int32, out_ref.shape, 0)
    out_ref[...] = jnp.where(row == 0, more, units).astype(jnp.float32)


def needs(mask):
    return pl.pallas_call(
        needs_kernel,
        out_shape=jax.ShapeDtypeStruct((8, 128), jnp.float32),
        in_specs=[SMEM],
        out_specs=VMEM,
        cost_estimate=COST,
        name="needs",
    )(mask)


def pack_kernel(place_ref, mask_ref, integrals_ref, *out_refs):
    block = place_ref[0]
    rank = jnp.int32(0)
    for jj in range(2):

        def step(i, rank, jj=jj):
            kept = mask_ref[i, 2 * block + jj]
            row = pl.ds(pl.multiple_of(i * TILE, TILE), TILE)

            @pl.when(kept == 1)
            def _():
                tile = jnp.swapaxes(integrals_ref[row, pl.ds(jj * TILE, TILE)], 0, 1)
                head_ref, most_ref, last_ref = out_refs
                most = most_ref.shape[0]

                @pl.when(rank < HEAD)
                def _():
                    head_ref[rank] = tile

                @pl.when(rank < most)
                def _():
                    most_ref[rank] = tile

                @pl.when(rank >= most)
                def _():
                    last_ref[rank - most] = tile

            return rank + kept

        rank = lax.fori_loop(0, mask_ref.shape[0], step, rank)


def pack(place, mask, integrals):
    sizes = [HEAD, HEAD + GROUP, 2 * mask.shape[0] - HEAD - GROUP]
    shapes = [jax.ShapeDtypeStruct((size, TILE, TILE), jnp.float32) for size in sizes]
    return pl.pallas_call(
        pack_kernel,
        out_shape=shapes,
        in_specs=[SMEM, SMEM, VMEM],
        out_specs=[VMEM] * len(shapes),
        compiler_params=pltpu.CompilerParams(vmem_limit_bytes=VMEM_LIMIT),
        cost_estimate=COST,
        name="pack",
    )(place, mask, integrals)


def rest_kernel(n_mine, place_ref, first_ref, mask_ref, *refs):
    out_ref, held, sem = refs[-3:]
    first, slots = first_ref[0], out_ref.shape[0]
    start = -first
    blocks = (refs[:n_mine], refs[n_mine : 2 * n_mine])
    copies = []
    for which in range(2):
        to = 0
        for part, ref in enumerate(blocks[which]):
            skip = HEAD if part == 0 else 0
            size = ref.shape[0] - skip
            copy = pltpu.make_async_copy(
                ref.at[pl.ds(skip, size)], held.at[which, pl.ds(to, size)], sem.at[len(copies)]
            )
            copy.start()
            copies.append(copy)
            to += size
    for copy in copies:
        copy.wait()
    for which in range(2):
        count = jnp.maximum(kept_in_block(mask_ref, place_ref[which]) - HEAD, 0)
        for k in range(held.shape[1]):
            to = start + k

            @pl.when((k < count) & (to >= 0) & (to < slots))
            def _(k=k, to=to, which=which):
                out_ref[to] = held[which, k]

        start = start + count


def rest(place, first, mask, mine, other, slots, *earlier):
    size = sum(part.shape[0] for part in mine) - HEAD
    return pl.pallas_call(
        functools.partial(rest_kernel, len(mine)),
        out_shape=jax.ShapeDtypeStruct((slots, TILE, TILE), jnp.float32),
        in_specs=[SMEM] * 3 + [ANY] * (len(mine) + len(other) + len(earlier)),
        out_specs=VMEM,
        scratch_shapes=[
            pltpu.VMEM((2, size, TILE, TILE), jnp.float32),
            pltpu.SemaphoreType.DMA((2 * len(mine),)),
        ],
        compiler_params=pltpu.CompilerParams(vmem_limit_bytes=VMEM_LIMIT),
        cost_estimate=COST,
        name="rest",
    )(place, first, mask, *mine, *other, *earlier)


def room(shapes):
    return pl.pallas_call(
        lambda *refs: None,
        out_shape=[jax.ShapeDtypeStruct(shape, jnp.float32) for shape in shapes],
        out_specs=[ANY] * len(shapes),
        name="room",
    )()


def split(x):
    high = x.astype(jnp.bfloat16)
    return high, (x - high.astype(jnp.float32)).astype(jnp.bfloat16)


def split_kernel(x_ref, *refs):
    high_ref, low_ref, held, sem = refs[-4:]
    parts = held.shape[0]
    size = held.shape[1]
    copies = [
        pltpu.make_async_copy(x_ref.at[pl.ds(k * size, size)], held.at[k], sem.at[k]) for k in range(parts)
    ]
    for copy in copies:
        copy.start()
    for k in range(parts):
        copies[k].wait()
        rows = pl.ds(k * size, size)
        high_ref[rows], low_ref[rows] = split(held[k])


def split_array(x, *earlier):
    parts = 8
    shape = pltpu.VMEM(x.shape, jnp.bfloat16)
    return pl.pallas_call(
        split_kernel,
        out_shape=[shape, shape],
        in_specs=[ANY] * (1 + len(earlier)),
        out_specs=[VMEM, VMEM],
        scratch_shapes=[
            pltpu.VMEM((parts, x.shape[0] // parts, x.shape[1]), jnp.float32),
            pltpu.SemaphoreType.DMA((parts,)),
        ],
        compiler_params=pltpu.CompilerParams(vmem_limit_bytes=VMEM_LIMIT),
        cost_estimate=COST,
        name="split",
    )(x, *earlier)


def stage_kernel(sizes, place_ref, mask_ref, high_ref, low_ref, *refs):
    n_mine, n_other, n_rest = sizes
    mine_refs, refs = refs[:n_mine], refs[n_mine:]
    other_refs, refs = refs[:n_other], refs[n_other:]
    rest_refs = refs[:n_rest]
    keep_ref, send_ref, held, sem, i_low, i_high, out, out_sem = refs[-8:]
    rows_t = mask_ref.shape[0]
    stride = held.shape[0] // 2
    chunks, depth, width = i_low.shape[0], i_low.shape[2], high_ref.shape[1]
    step = 256
    core = place_ref[2]

    copies = []

    def bring(ref, start):
        copy = pltpu.make_async_copy(ref, held.at[pl.ds(start, ref.shape[0])], sem.at[len(copies)])
        copy.start()
        copies.append(copy)

    for which, block_refs in enumerate((mine_refs, other_refs)):
        start = which * stride
        for ref in block_refs:
            bring(ref, start)
            start += ref.shape[0]
        if n_rest:
            bring(rest_refs[0], start)
    ranks, totals = [], []
    for which in range(2):
        counts = []
        for jj in range(2):
            count = jnp.int32(0)
            for i in range(rows_t):
                count = count + mask_ref[i, 2 * place_ref[which] + jj]
            counts.append(count)
        ranks += [jnp.int32(0), counts[0]]
        totals.append(counts[0] + counts[1])
    extra = jnp.maximum(totals[0] - HEAD, 0) if n_rest else jnp.int32(0)
    for copy in copies:
        copy.wait()
    if n_rest:

        @pl.when(extra + jnp.maximum(totals[1] - HEAD, 0) > GROUP)
        def _():
            spilled = []
            for which in range(2):
                to = held.at[pl.ds(which * stride + HEAD + GROUP, rest_refs[1].shape[0])]
                spilled.append(pltpu.make_async_copy(rest_refs[1], to, sem.at[which]))
            for copy in spilled:
                copy.start()
            for copy in spilled:
                copy.wait()

    def unpack(k, ranks):
        ranks = list(ranks)
        for q in range(4):
            which, jj = q // 2, q % 2
            rows = pl.ds(q * TILE, TILE)
            for part in range(depth // TILE):
                kept = mask_ref[k * (depth // TILE) + part, 2 * place_ref[which] + jj]
                slot = jnp.where(ranks[q] < HEAD, ranks[q], ranks[q] + (extra if which else 0))
                slot = which * stride + jnp.minimum(slot, stride - 1)
                high, low = split(jnp.where(kept == 1, held[slot], 0.0))
                columns = pl.ds(part * TILE, TILE)
                i_high[k, rows, columns] = high
                i_low[k, rows, columns] = low
                ranks[q] = ranks[q] + kept
        return tuple(ranks)

    lax.fori_loop(0, chunks, unpack, tuple(ranks))

    def dot(a, b):
        return jnp.dot(a, b, preferred_element_type=jnp.float32)

    def out_copies(n):
        columns = pl.ds(pl.multiple_of(n * step, step), step)
        return [
            pltpu.make_async_copy(out.at[part, :, columns], ref.at[:, columns], out_sem.at[n, part])
            for part, ref in enumerate((keep_ref, send_ref))
        ]

    def product(n, carry):
        columns = pl.ds(pl.multiple_of(n * step, step), step)
        total = None
        for k in range(chunks):
            high = high_ref[pl.ds(k * depth, depth), columns]
            low = low_ref[pl.ds(k * depth, depth), columns]
            left = jnp.concatenate([i_low[k], i_high[k], i_high[k]], axis=1)
            part = dot(left, jnp.concatenate([high, low, high], axis=0))
            total = part if total is None else total + part
        first = jnp.concatenate([total[:TILE], total[2 * TILE : 3 * TILE]], axis=0)
        second = jnp.concatenate([total[TILE : 2 * TILE], total[3 * TILE :]], axis=0)
        out[0, :, columns] = jnp.where(core == 0, first, second)
        out[1, :, columns] = jnp.where(core == 0, second, first)
        for copy in out_copies(n):
            copy.start()
        return carry

    lax.fori_loop(0, width // step, product, 0)
    for n in range(width // step):
        for copy in out_copies(n):
            copy.wait()


def stage(place, mask, high, low, mine, other, rests, cost, earlier):
    rows, width = high.shape
    depth = 256
    half = pltpu.HBM((2 * TILE, width), jnp.float32)
    tiles = list(mine) + list(other) + list(rests)
    return pl.pallas_call(
        functools.partial(stage_kernel, (len(mine), len(other), len(rests))),
        out_shape=[half, half],
        in_specs=[SMEM, SMEM, VMEM, VMEM] + [HBM] * (len(tiles) + len(earlier)),
        out_specs=[ANY, ANY],
        scratch_shapes=[
            pltpu.VMEM((2 * (HEAD + 2 * mask.shape[0]), TILE, TILE), jnp.float32),
            pltpu.SemaphoreType.DMA((len(tiles) + 1,)),
            pltpu.VMEM((rows // depth, 4 * TILE, depth), jnp.bfloat16),
            pltpu.VMEM((rows // depth, 4 * TILE, depth), jnp.bfloat16),
            pltpu.VMEM((2, 2 * TILE, width), jnp.float32),
            pltpu.SemaphoreType.DMA((width // 256, 2)),
        ],
        compiler_params=pltpu.CompilerParams(vmem_limit_bytes=VMEM_LIMIT),
        cost_estimate=cost,
        name="stage",
    )(place, mask, *(pltpu.with_memory_space_constraint(a, pltpu.VMEM) for a in (high, low)), *tiles, *earlier)


def met(*arrays):
    return pl.pallas_call(
        lambda *refs: None,
        out_shape=jax.ShapeDtypeStruct((8, 128), jnp.float32),
        in_specs=[ANY] * len(arrays),
        out_specs=ANY,
        name="met",
    )(*arrays)


def add_kernel(a_ref, b_ref, *refs):
    refs[-1][...] = a_ref[...] + b_ref[...]


def add(a, b, *earlier):
    step = a.shape[0] // 2
    spec = pl.BlockSpec((step, a.shape[1]), lambda i: (i, 0))
    return pl.pallas_call(
        add_kernel,
        grid=(a.shape[0] // step,),
        out_shape=pltpu.HBM(a.shape, a.dtype),
        in_specs=[spec, spec] + [ANY] * len(earlier),
        out_specs=spec,
        compiler_params=pltpu.CompilerParams(vmem_limit_bytes=VMEM_LIMIT),
        cost_estimate=COST,
        name="add",
    )(a, b, *earlier)


def pass_kernel(turn_ref, *refs):
    pieces, (out_ref, held, sem) = refs[:-4], refs[-3:]
    for s in range(len(pieces) // 2):

        @pl.when(turn_ref[0] == s)
        def _():
            copies = [pltpu.make_async_copy(pieces[2 * s + k], held.at[k], sem.at[k]) for k in range(2)]
            for copy in copies:
                copy.start()
            for copy in copies:
                copy.wait()
            out_ref[...] = held[0] + held[1]


def to_pass(turn, pieces, later):
    shape = pieces[0][0].shape
    flat = [piece for pair in pieces for piece in pair]
    return pl.pallas_call(
        pass_kernel,
        out_shape=jax.ShapeDtypeStruct(shape, jnp.float32),
        in_specs=[SMEM] + [HBM] * len(flat) + [ANY],
        out_specs=VMEM,
        scratch_shapes=[pltpu.VMEM((2,) + shape, jnp.float32), pltpu.SemaphoreType.DMA((2,))],
        compiler_params=pltpu.CompilerParams(vmem_limit_bytes=VMEM_LIMIT),
        cost_estimate=COST,
        name="pass",
    )(turn, *flat, later)


def finish_kernel(counts, place_ref, base_ref, vir_ref, occ_ref, *refs):
    pieces, refs = refs[: sum(counts)], refs[sum(counts) :]
    residual_ref, update_ref, held, sem = refs
    core, y, turn = place_ref[0], place_ref[1], place_ref[2]
    start = 0
    for s, count in enumerate(counts):

        @pl.when(turn == s)
        def _(start=start, count=count):
            copies = [pltpu.make_async_copy(pieces[start + k], held.at[k], sem.at[k]) for k in range(count)]
            for copy in copies:
                copy.start()
            for copy in copies:
                copy.wait()
            for k in range(count, 4):
                held[k] = jnp.zeros(held.shape[1:], jnp.float32)

        start += count
    for half in range(2):
        for which in range(2):
            block = y if which == 0 else 1 - y
            tile = core if half == 0 else 1 - core
            rows = pl.ds(pl.multiple_of(block * 2 * TILE + tile * TILE, TILE), TILE)
            part = pl.ds(which * TILE, TILE)
            ladder = held[2 * half, part] + held[2 * half + 1, part]
            residual = base_ref[rows] + ladder
            residual_ref[rows] = residual
            update_ref[rows] = residual / (vir_ref[rows] + occ_ref[...])


def finish(place, base, vir, occ, pieces):
    shape = jax.ShapeDtypeStruct(base.shape, jnp.float32)
    flat = [piece for stage_pieces in pieces for piece in stage_pieces]
    return pl.pallas_call(
        functools.partial(finish_kernel, tuple(len(p) for p in pieces)),
        out_shape=[shape, shape],
        in_specs=[SMEM, VMEM, VMEM, VMEM] + [HBM] * len(flat),
        out_specs=[VMEM, VMEM],
        scratch_shapes=[
            pltpu.VMEM((4,) + flat[0].shape, jnp.float32),
            pltpu.SemaphoreType.DMA((4,)),
        ],
        compiler_params=pltpu.CompilerParams(vmem_limit_bytes=VMEM_LIMIT),
        cost_estimate=COST,
        name="finish",
    )(place, base, vir, occ, *flat)


def planned(amplitudes, integrals, screen_mask, base_residual, vir_energy, occ_energy):
    both = ("row", "loop")
    zs = range(4)
    row, loop = lax.axis_index("row"), lax.axis_index("loop")
    core, z, y = row % 2, loop // 2, loop % 2
    mask = screen_mask

    def around(x, steps=1):
        return lax.ppermute(x, "loop", [(2 * a + b, 2 * ((a + steps) % 4) + b) for a in zs for b in range(2)])

    def across(x):
        return lax.ppermute(x, "loop", [(a, a ^ 1) for a in range(8)])

    def cores(x):
        return lax.ppermute(x, "row", [(0, 1), (1, 0), (2, 3), (3, 2)])

    def chips(x):
        return lax.ppermute(x, "row", [(0, 2), (2, 0), (1, 3), (3, 1)])

    def to_owner(x, s, flip):
        pairs = [
            ((((a - s) % 4) ^ flip) * 8 + 2 * a + b, ((a - s) % 4) * 8 + 2 * a + b) for a in zs for b in range(2)
        ]
        return lax.ppermute(x, both, pairs)

    def to_chip(x, s):
        pairs = [
            ((((a - s) % 4) ^ c ^ 2) * 8 + 2 * a + b, (((a - s) % 4) ^ c) * 8 + 2 * a + b)
            for a in zs
            for b in range(2)
            for c in range(2)
        ]
        return lax.ppermute(x, both, pairs)

    def place_of(s):
        pair = 2 * ((z - s) % 4)
        return jnp.stack([pair + y, pair + 1 - y, core]).astype(jnp.int32)

    def after(x, *others):
        return lax.optimization_barrier((x, *others))[0]

    def partial(s, cost, mine, other, rests, *earlier):
        return stage(places[s], mask, high, low, mine, other, rests, cost, earlier)

    head, most, last = pack(place_of(0), mask, integrals)
    first_need = needs(after(mask, last))
    need = jnp.maximum(first_need, cores(first_need))
    need = jnp.maximum(need, chips(need)).astype(jnp.int32)
    more, units = need[0, 0], need[1, 0]

    head1 = around(head)
    other_most = across(most)
    zero = jnp.zeros((1,), jnp.int32)
    head2 = around(head1)
    crossed1 = across(head1)
    mixed = rest(place_of(0), zero, mask, [most], [other_most], GROUP, head1)
    rest1 = around(mixed)

    spare = room([last.shape] + [(2 * mask.shape[0] - GROUP, TILE, TILE)] * 3)

    def send_last(carry):
        done, tiles = lax.optimization_barrier((carry[0], last))
        return done + 1, across(tiles)

    more = after(more, mixed)
    other_last = lax.while_loop(lambda c: c[0] < more, send_last, (jnp.int32(0), spare[0]))[1]

    def spill(carry):
        unit, held = carry[0], carry[1:]
        first = (GROUP + UNIT * unit)[None]
        tiles = rest(place_of(0), first, mask, [most, last], [other_most, other_last], UNIT)
        moved = [around(tiles, s) for s in (1, 2, 3)]
        held = [lax.dynamic_update_slice(h, m, (UNIT * unit, 0, 0)) for h, m in zip(held, moved)]
        return (unit + 1, *held)

    units = after(units, mixed)
    spilled = lax.while_loop(lambda c: c[0] < units, spill, (jnp.int32(0), *spare[1:]))[1:]

    places = [place_of(s) for s in range(4)]
    turn = ((z - (row ^ 1)) % 4).astype(jnp.int32)[None]
    place = jnp.stack([core, y, (z - row) % 4]).astype(jnp.int32)
    vir, occ = vir_energy[:, None], occ_energy[None, :]
    high, low = split_array(after(amplitudes, spilled[0], other_last), *places, turn, place, vir, occ)

    keep0, send0 = partial(0, STAGE_COST, [most, last], [other_most, other_last], [])
    total0 = add(keep0, cores(send0))
    moved0 = to_chip(total0, 0)

    head3 = around(head2)
    crossed2 = across(head2)
    rest2 = around(rest1)
    keep1, send1 = partial(1, STAGE_COST, [head1], [crossed1], [rest1, spilled[0]], head2)
    total1 = add(keep1, cores(after(send1, crossed2, total0)))
    moved1 = to_chip(total1, 1)
    crossed3 = across(head3)
    rest3 = around(rest2)

    keep2, send2 = partial(2, COST, [head2], [crossed2], [rest2, spilled[1]], head3, total1)
    total2 = add(keep2, cores(after(send2, rest3, crossed3, moved0, moved1)))
    moved2 = to_chip(total2, 2)

    keep3, send3 = partial(3, STAGE_COST, [head3], [crossed3], [rest3, spilled[2]], total2)
    total3 = add(keep3, cores(after(send3)))
    pieces = [(total0, moved0), (total1, moved1), (total2, moved2)]
    passed = cores(to_pass(turn, pieces, moved2))
    pieces = [pair + (passed,) for pair in pieces]
    pieces.append((total3, to_owner(total3, 3, 2), to_owner(total3, 3, 3), to_owner(total3, 3, 1)))
    return tuple(finish(place, base_residual, vir, occ, pieces))


def solution(mesh):
    in_specs = (
        P("row", "loop"),
        P("row", "loop"),
        P("row", None),
        P("row", "loop"),
        P("row"),
        P("loop"),
    )
    out_specs = (P("row", "loop"), P("row", "loop"))
    body = planned if (mesh.shape["row"], mesh.shape["loop"]) == (4, 8) else gathered
    return jax.shard_map(body, mesh=mesh, in_specs=in_specs, out_specs=out_specs, check_vma=False)
```

time: 363 us -> 184 us (0.51)
  waiting for transfers between devices: 287 us -> 93.8 us
  matrix products: 54 us -> 0 us
  Pallas kernels: 0 us -> 51.2 us
  starting transfers between devices: 0.08 us -> 25.1 us
  between operations: 14 us -> 1.05 us
  local copies, waits for them, and re-layouts: 1.15 us -> 9.7 us
    all_gather x1 -> x0, waiting for transfers between devices: 228 us -> none  [on_device(): assembled = lax.all_gather(integrals, 'loop', axis=1, tiled=True)]
    ppermute x0 -> x23, waiting for transfers between devices: none -> 93.8 us  [the longest x6 27.4 us: around(): lax.ppermute(x, 'loop', [(2 * a + b, 2 * ((a + steps) % 4) + b) for a in...]
    reduce_scatter x1 -> x0, waiting for transfers between devices: 57.6 us -> none  [on_device(): lax.psum_scatter(contract(screened, amplitudes), 'row', scatter_dimension...]
    dot_general x1 -> x0, matrix products: 54 us -> none  [contract(): lax.dot_general(panel, amplitudes, (((0,), (0,)), ((), ())), precision=la...]
    pallas_call x0 -> x15, Pallas kernels: none -> 51.2 us  [the longest x4 35.2 us: stage(): pl.pallas_call(functools.partial(stage_kernel, (len(mine), len(other), le...]
    ppermute x0 -> x23, starting transfers between devices: none -> 25.1 us  [the longest x6 9.1 us: around(): lax.ppermute(x, 'loop', [(2 * a + b, 2 * ((a + steps) % 4) + b) for a in...]
    unnamed x6 -> x40, local copies, waits for them, and re-layouts: 0.01 us -> 8.97 us
  transfers between devices with their start and end apart: 2 -> 23, of which waited for: 2 -> 14; matrix products, arithmetic and copies ran while one was open for 0% -> 1% of each run, Pallas kernels for 0% -> 24%
where the time goes in v1:
time: 184 us; the launch traced here: 183 us
  waiting for transfers between devices  93.8 us (51%)
  Pallas kernels  51.2 us (28%)
  starting transfers between devices  25.1 us (14%)
  local copies, waits for them, and re-layouts  9.7 us (5%)
    pallas_call x4, Pallas kernels, stage(): pl.pallas_call(functools.partial(stage_kernel, (len(mine), len(other), le...  35.2 us
    ppermute x6, waiting for transfers between devices, around(): lax.ppermute(x, 'loop', [(2 * a + b, 2 * ((a + steps) % 4) + b) for a in...  27.4 us
    ppermute x3, waiting for transfers between devices, to_chip(): return lax.ppermute(x, both, pairs)  22.3 us
    ppermute x4, waiting for transfers between devices, across(): return lax.ppermute(x, 'loop', [(a, a ^ 1) for a in range(8)])  19.6 us
    ppermute x3, waiting for transfers between devices, to_owner(): return lax.ppermute(x, both, pairs)  18.6 us
    ppermute x6, starting transfers between devices, around(): lax.ppermute(x, 'loop', [(2 * a + b, 2 * ((a + steps) % 4) + b) for a in...  9.1 us
    unnamed x40, local copies, waits for them, and re-layouts  8.97 us
    ppermute x4, starting transfers between devices, across(): return lax.ppermute(x, 'loop', [(a, a ^ 1) for a in range(8)])  5.4 us
  transfers between devices with their start and end apart: 23, of which 14 were waited for; matrix products, arithmetic and copies ran while one was open for 1% of the time, Pallas kernels for 24%

profile of v1, /device:TPU:10, one launch (start us, length us, event | category | flops | bytes accessed | tf_op | source)
XLA Modules:
  0.0 183.3 jit_solution(17224419614114330930)
XLA Ops:
  2.4 4.0 %pack.1 = (f32[16,128,128]{2,1,0:T(8,128)S(1)}, f32[24,128,128]{2,1,0:T(8,128)}, f32[8,128,128]{2,1,0:T(8,128)}) custom-call(s32[3]{0:T(128)S(1)} %add_add_fusion.place_ref.refs_0_, s32[16,16]{1,0:T(8,128)} %mask_ref.12, f32[2048,256]{1,0:T(8,128)S(1)} %copy-done.6), custom_call_target="tpu_custom_call" | custom-call | flops 1 | bytes 1 | tf_op jit(solution)/shard_map/pack/pallas_call | solution.py:116
  6.4 2.2 %collective-permute-start.6 = (f32[24,128,128]{2,1,0:T(8,128)}, f32[24,128,128]{2,1,0:T(8,128)}, u32[]{:S(2)}, u32[]{:S(2)}) collective-permute-start(f32[24,128,128]{2,1,0:T(8,128)} %get-tuple-element.381.refs_0_), channel_id=1, source_target_pairs={{0,1},{1,0},{2,3},{3,2},{4,5},{5,4},{6,7},{7,6},{8,9},{9,8},{10,11... | collective-permute-start | bytes 4718600 | tf_op jit(solution)/shard_map/ppermute | solution.py:466
  14.5 2.2 %collective-permute-done.5 = f32[8,128]{1,0:T(8,128)S(1)} collective-permute-done((f32[8,128]{1,0:T(8,128)S(1)}, f32[8,128]{1,0:T(8,128)S(1)}, u32[]{:S(2)}, u32[]{:S(2)}) %collective-permute-start.5) | collective-permute-done | bytes 4128 | tf_op jit(solution)/shard_map/ppermute | solution.py:472
  17.4 15.4 %collective-permute-done.7.refs_2_.refs_0_ = f32[16,128,128]{2,1,0:T(8,128)S(1)} collective-permute-done((f32[16,128,128]{2,1,0:T(8,128)S(1)}, f32[16,128,128]{2,1,0:T(8,128)S(1)}, u32[]{:S(2)}, u32[]{:S(2)}) %collective-permute-start.7) | collective-permute-done | bytes 1048608 | tf_op jit(solution)/shard_map/ppermute | solution.py:463
  34.7 9.4 %collective-permute-done.6.refs_1_.refs_2_ = f32[24,128,128]{2,1,0:T(8,128)} collective-permute-done((f32[24,128,128]{2,1,0:T(8,128)}, f32[24,128,128]{2,1,0:T(8,128)}, u32[]{:S(2)}, u32[]{:S(2)}) %collective-permute-start.6) | collective-permute-done | bytes 1572896 | tf_op jit(solution)/shard_map/ppermute | solution.py:466
  44.1 1.9 %rest.4 = f32[8,128,128]{2,1,0:T(8,128)S(1)} custom-call(s32[3]{0:T(128)S(1)} %add_add_fusion.place_ref.refs_0_, s32[1]{0:T(128)} %constant.113.clone.1.first_ref, s32[16,16]{1,0:T(8,128)S(1)} %copy-done.15, f32[24,128,128]{2,1,0:T(8,128)} %get-tuple-element.381.refs_0_, f32[24,128,128]{2,1,0:T(8,128)} %collective-permute-done.6.refs_1_.refs_2_, ...), custom_call_target="tpu_custom_call" | custom-call | flops 1 | bytes 1 | tf_op jit(solution)/shard_map/rest/pallas_call | solution.py:160
  47.4 2.2 %collective-permute-start.11 = (f32[8,128,128]{2,1,0:T(8,128)S(1)}, f32[8,128,128]{2,1,0:T(8,128)S(1)}, u32[]{:S(2)}, u32[]{:S(2)}) collective-permute-start(f32[8,128,128]{2,1,0:T(8,128)S(1)} %rest.4), channel_id=1, source_target_pairs={{0,2},{1,3},{2,4},{3,5},{4,6},{5,7},{6,0},{7,1},{8,10},{9,11},{10,... | collective-permute-start | bytes 1572872 | tf_op jit(solution)/shard_map/ppermute | solution.py:463
  49.6 2.8 %copy-done.4 = f32[2048,768]{1,0:T(8,128)S(1)} copy-done((f32[2048,768]{1,0:T(8,128)S(1)}, f32[2048,768]{1,0:T(8,128)}, u32[]{:S(2)}) %copy-start.4) | copy-done | bytes 6291480
  54.0 9.9 %stage.4 = (f32[256,768]{1,0:T(8,128)}, f32[256,768]{1,0:T(8,128)}) custom-call(s32[3]{0:T(128)S(1)} %get-tuple-element.464, s32[16,16]{1,0:T(8,128)S(1)} %get-tuple-element.463, bf16[2048,768]{1,0:T(8,128)(2,1)S(1)} %get-tuple-element.217.high_ref, bf16[2048,768]{1,0:T(8,128)(2,1)S(1)} %get-tuple-element.218.low_ref, ...), custom_call_target="tpu_custom_call" | custom-call | flops 46000001024 | bytes 1 | tf_op jit(solution)/shard_map/stage/pallas_call | solution.py:330
  64.9 2.2 %collective-permute-start.17 = (f32[16,128,128]{2,1,0:T(8,128)S(1)}, f32[16,128,128]{2,1,0:T(8,128)S(1)}, u32[]{:S(2)}, u32[]{:S(2)}) collective-permute-start(f32[16,128,128]{2,1,0:T(8,128)S(1)} %collective-permute-done.12.refs_4_.refs_0_), channel_id=1, source_target_pairs={{0,2},{1,3},{2,4},{3,5},{4,6},{5,7},{6,0},{7,1},{8,10},{9,11},{10,... | collective-permute-start | bytes 3145736 | tf_op jit(solution)/shard_map/ppermute | solution.py:463
  67.1 2.1 %collective-permute-done.11.refs_2_ = f32[8,128,128]{2,1,0:T(8,128)S(1)} collective-permute-done((f32[8,128,128]{2,1,0:T(8,128)S(1)}, f32[8,128,128]{2,1,0:T(8,128)S(1)}, u32[]{:S(2)}, u32[]{:S(2)}) %collective-permute-start.11) | collective-permute-done | bytes 524320 | tf_op jit(solution)/shard_map/ppermute | solution.py:463
  69.2 9.2 %stage.5 = (f32[256,768]{1,0:T(8,128)}, f32[256,768]{1,0:T(8,128)}) custom-call(s32[3]{0:T(128)S(1)} %add_add_fusion.1.refs_1_.place_ref, s32[16,16]{1,0:T(8,128)S(1)} %get-tuple-element.463, bf16[2048,768]{1,0:T(8,128)(2,1)S(1)} %get-tuple-element.217.high_ref, bf16[2048,768]{1,0:T(8,128)(2,1)S(1)} %get-tuple-element.218.low_ref, ...), custom_call_target="tpu_custom_call" | custom-call | flops 46000001024 | bytes 1 | tf_op jit(solution)/shard_map/stage/pallas_call | solution.py:330
  79.4 10.2 %collective-permute-done.13.refs_1_ = f32[16,128,128]{2,1,0:T(8,128)S(1)} collective-permute-done((f32[16,128,128]{2,1,0:T(8,128)S(1)}, f32[16,128,128]{2,1,0:T(8,128)S(1)}, u32[]{:S(2)}, u32[]{:S(2)}) %collective-permute-start.13) | collective-permute-done | bytes 1048608 | tf_op jit(solution)/shard_map/ppermute | solution.py:466
  90.9 1.7 collective-permute-start.19
  92.6 2.7 %collective-permute-start.9 = (f32[256,768]{1,0:T(8,128)}, f32[256,768]{1,0:T(8,128)S(1)}, u32[]{:S(2)}, u32[]{:S(2)}) collective-permute-start(f32[256,768]{1,0:T(8,128)} %add.137.refs_0_), channel_id=1, source_target_pairs={{16,0},{24,8},{17,1},{25,9},{26,10},{18,2},{27,11},{19,3},{4,20},{... | collective-permute-start | bytes 2359304 | tf_op jit(solution)/shard_map/ppermute | solution.py:487
  97.6 6.3 %collective-permute-done.16.refs_2_ = f32[8,128,128]{2,1,0:T(8,128)S(1)} collective-permute-done((f32[8,128,128]{2,1,0:T(8,128)S(1)}, f32[8,128,128]{2,1,0:T(8,128)S(1)}, u32[]{:S(2)}, u32[]{:S(2)}) %collective-permute-start.16) | collective-permute-done | bytes 524320 | tf_op jit(solution)/shard_map/ppermute | solution.py:463
  106.3 8.1 %stage.6 = (f32[256,768]{1,0:T(8,128)}, f32[256,768]{1,0:T(8,128)}) custom-call(s32[3]{0:T(128)S(1)} %add_add_fusion.2.refs_2_.place_ref, s32[16,16]{1,0:T(8,128)S(1)} %get-tuple-element.463, bf16[2048,768]{1,0:T(8,128)(2,1)S(1)} %get-tuple-element.217.high_ref, bf16[2048,768]{1,0:T(8,128)(2,1)S(1)} %get-tuple-element.218.low_ref, ...), custom_call_target="tpu_custom_call" | custom-call | flops 1 | bytes 1 | tf_op jit(solution)/shard_map/stage/pallas_call | solution.py:330
  114.4 3.4 %collective-permute-done.18.refs_2_ = f32[8,128,128]{2,1,0:T(8,128)S(1)} collective-permute-done((f32[8,128,128]{2,1,0:T(8,128)S(1)}, f32[8,128,128]{2,1,0:T(8,128)S(1)}, u32[]{:S(2)}, u32[]{:S(2)}) %collective-permute-start.18) | collective-permute-done | bytes 524320 | tf_op jit(solution)/shard_map/ppermute | solution.py:463
  117.8 11.4 %collective-permute-done.15.refs_3_.refs_4_ = f32[256,768]{1,0:T(8,128)S(1)} collective-permute-done((f32[256,768]{1,0:T(8,128)}, f32[256,768]{1,0:T(8,128)S(1)}, u32[]{:S(2)}, u32[]{:S(2)}) %collective-permute-start.15) | collective-permute-done | bytes 786464 | tf_op jit(solution)/shard_map/ppermute | solution.py:487
  129.3 2.5 %collective-permute-done.20.b_ref = f32[256,768]{1,0:T(8,128)S(1)} collective-permute-done((f32[256,768]{1,0:T(8,128)}, f32[256,768]{1,0:T(8,128)S(1)}, u32[]{:S(2)}, u32[]{:S(2)}) %collective-permute-start.20) | collective-permute-done | bytes 786464 | tf_op jit(solution)/shard_map/ppermute | solution.py:469
  136.2 8.1 %stage.7 = (f32[256,768]{1,0:T(8,128)}, f32[256,768]{1,0:T(8,128)}) custom-call(s32[3]{0:T(128)S(1)} %add_add_fusion.3.refs_3_.place_ref, s32[16,16]{1,0:T(8,128)S(1)} %get-tuple-element.463, bf16[2048,768]{1,0:T(8,128)(2,1)S(1)} %get-tuple-element.217.high_ref, bf16[2048,768]{1,0:T(8,128)(2,1)S(1)} %get-tuple-element.218.low_ref, ...), custom_call_target="tpu_custom_call" | custom-call | flops 46000001024 | bytes 1 | tf_op jit(solution)/shard_map/stage/pallas_call | solution.py:330
  144.6 10.9 %collective-permute-done.21.refs_5_.refs_6_.refs_7_ = f32[256,768]{1,0:T(8,128)S(1)} collective-permute-done((f32[256,768]{1,0:T(8,128)}, f32[256,768]{1,0:T(8,128)S(1)}, u32[]{:S(2)}, u32[]{:S(2)}) %collective-permute-start.21) | collective-permute-done | bytes 786464 | tf_op jit(solution)/shard_map/ppermute | solution.py:487
  160.7 17.9 %collective-permute-done.24.refs_10_ = f32[256,768]{1,0:T(8,128)S(1)} collective-permute-done((f32[256,768]{1,0:T(8,128)}, f32[256,768]{1,0:T(8,128)S(1)}, u32[]{:S(2)}, u32[]{:S(2)}) %collective-permute-start.24) | collective-permute-done | bytes 786464 | tf_op jit(solution)/shard_map/ppermute | solution.py:478
  180.4 2.9 %finish.1 = (f32[512,768]{1,0:T(8,128)}, f32[512,768]{1,0:T(8,128)}) custom-call(s32[3]{0:T(128)S(1)} %pad_add_fusion.refs_5_.place_ref, f32[512,768]{1,0:T(8,128)S(1)} %copy-done.7, f32[512,1]{1,0:T(8,128)S(1)} %copy.9.refs_6_.vir_ref, f32[1,768]{1,0:T(1,128)S(1)} %broadcast_in_dim.13.refs_7_.occ_ref, f32[256,768]{1,0:T(8,128)S(1)} %copy-done.2, ...), custom_call_target="tpu_custom_call" | custom-call | flops 1 | bytes 1 | tf_op jit(solution)/shard_map/finish/pallas_call | solution.py:440
  (89 shorter events, 32.7 us)
Async XLA Ops:
  6.4 37.7 %collective-permute-start.6 = (f32[24,128,128]{2,1,0:T(8,128)}, f32[24,128,128]{2,1,0:T(8,128)}, u32[]{:S(2)}, u32[]{:S(2)}) collective-permute-start(f32[24,128,128]{2,1,0:T(8,128)} %get-tuple-element.381.refs_0_), channel_id=1, source_target_pairs={{0,1},{1,0},{2,3},{3,2},{4,5},{5,4},{6,7},{7,6},{8,9},{9,8},{10,11... | collective-permute-start | bytes 4718600 | tf_op jit(solution)/shard_map/ppermute | solution.py:466
  8.6 24.2 %collective-permute-start.7 = (f32[16,128,128]{2,1,0:T(8,128)S(1)}, f32[16,128,128]{2,1,0:T(8,128)S(1)}, u32[]{:S(2)}, u32[]{:S(2)}) collective-permute-start(f32[16,128,128]{2,1,0:T(8,128)S(1)} %get-tuple-element.210), channel_id=1, source_target_pairs={{0,2},{1,3},{2,4},{3,5},{4,6},{5,7},{6,0},{7,1},{8,10},{9,11},{10,... | collective-permute-start | bytes 3145736 | tf_op jit(solution)/shard_map/ppermute | solution.py:463
  11.1 1.4 collective-permute-start.4
  13.2 3.6 %collective-permute-start.5 = (f32[8,128]{1,0:T(8,128)S(1)}, f32[8,128]{1,0:T(8,128)S(1)}, u32[]{:S(2)}, u32[]{:S(2)}) collective-permute-start(f32[8,128]{1,0:T(8,128)S(1)} %max.6), channel_id=1, source_target_pairs={{0,16},{16,0},{8,24},{24,8},{1,17},{17,1},{9,25},{25,9},{2,18},{18... | collective-permute-start | bytes 12296 | tf_op jit(solution)/shard_map/ppermute | solution.py:472
  32.7 34.3 %collective-permute-start.10 = (f32[16,128,128]{2,1,0:T(8,128)S(1)}, f32[16,128,128]{2,1,0:T(8,128)}, u32[]{:S(2)}, u32[]{:S(2)}) collective-permute-start(f32[16,128,128]{2,1,0:T(8,128)S(1)} %collective-permute-done.7.refs_2_.refs_0_), channel_id=1, source_target_pairs={{0,1},{1,0},{2,3},{3,2},{4,5},{5,4},{6,7},{7,6},{8,9},{9,8},{10,11... | collective-permute-start | bytes 3145736 | tf_op jit(solution)/shard_map/ppermute | solution.py:466
  33.4 30.6 %collective-permute-start.12 = (f32[16,128,128]{2,1,0:T(8,128)S(1)}, f32[16,128,128]{2,1,0:T(8,128)S(1)}, u32[]{:S(2)}, u32[]{:S(2)}) collective-permute-start(f32[16,128,128]{2,1,0:T(8,128)S(1)} %collective-permute-done.7.refs_2_.refs_0_), channel_id=1, source_target_pairs={{0,2},{1,3},{2,4},{3,5},{4,6},{5,7},{6,0},{7,1},{8,10},{9,11},{10,... | collective-permute-start | bytes 3145736 | tf_op jit(solution)/shard_map/ppermute | solution.py:463
  47.4 21.8 %collective-permute-start.11 = (f32[8,128,128]{2,1,0:T(8,128)S(1)}, f32[8,128,128]{2,1,0:T(8,128)S(1)}, u32[]{:S(2)}, u32[]{:S(2)}) collective-permute-start(f32[8,128,128]{2,1,0:T(8,128)S(1)} %rest.4), channel_id=1, source_target_pairs={{0,2},{1,3},{2,4},{3,5},{4,6},{5,7},{6,0},{7,1},{8,10},{9,11},{10,... | collective-permute-start | bytes 1572872 | tf_op jit(solution)/shard_map/ppermute | solution.py:463
  63.9 14.5 %collective-permute-start.8 = (f32[256,768]{1,0:T(8,128)}, f32[256,768]{1,0:T(8,128)S(1)}, u32[]{:S(2)}, u32[]{:S(2)}) collective-permute-start(f32[256,768]{1,0:T(8,128)} %get-tuple-element.220), channel_id=1, source_target_pairs={{0,8},{8,0},{16,24},{24,16},{1,9},{9,1},{17,25},{25,17},{2,10},{10... | collective-permute-start | bytes 2359304 | tf_op jit(solution)/shard_map/ppermute | solution.py:469
  64.0 25.6 %collective-permute-start.13 = (f32[16,128,128]{2,1,0:T(8,128)S(1)}, f32[16,128,128]{2,1,0:T(8,128)S(1)}, u32[]{:S(2)}, u32[]{:S(2)}) collective-permute-start(f32[16,128,128]{2,1,0:T(8,128)S(1)} %collective-permute-done.12.refs_4_.refs_0_), channel_id=1, source_target_pairs={{0,1},{1,0},{2,3},{3,2},{4,5},{5,4},{6,7},{7,6},{8,9},{9,8},{10,11... | collective-permute-start | bytes 3145736 | tf_op jit(solution)/shard_map/ppermute | solution.py:466
  64.9 26.0 %collective-permute-start.17 = (f32[16,128,128]{2,1,0:T(8,128)S(1)}, f32[16,128,128]{2,1,0:T(8,128)S(1)}, u32[]{:S(2)}, u32[]{:S(2)}) collective-permute-start(f32[16,128,128]{2,1,0:T(8,128)S(1)} %collective-permute-done.12.refs_4_.refs_0_), channel_id=1, source_target_pairs={{0,2},{1,3},{2,4},{3,5},{4,6},{5,7},{6,0},{7,1},{8,10},{9,11},{10,... | collective-permute-start | bytes 3145736 | tf_op jit(solution)/shard_map/ppermute | solution.py:463
  89.6 5.7 %collective-permute-start.14 = (f32[256,768]{1,0:T(8,128)S(1)}, f32[256,768]{1,0:T(8,128)S(1)}, u32[]{:S(2)}, u32[]{:S(2)}) collective-permute-start(f32[256,768]{1,0:T(8,128)S(1)} %copy-done.20), channel_id=1, source_target_pairs={{0,8},{8,0},{16,24},{24,16},{1,9},{9,1},{17,25},{25,17},{2,10},{10... | collective-permute-start | bytes 2359304 | tf_op jit(solution)/shard_map/ppermute | solution.py:469
  89.6 14.3 %collective-permute-start.16 = (f32[8,128,128]{2,1,0:T(8,128)S(1)}, f32[8,128,128]{2,1,0:T(8,128)S(1)}, u32[]{:S(2)}, u32[]{:S(2)}) collective-permute-start(f32[8,128,128]{2,1,0:T(8,128)S(1)} %collective-permute-done.11.refs_2_), channel_id=1, source_target_pairs={{0,2},{1,3},{2,4},{3,5},{4,6},{5,7},{6,0},{7,1},{8,10},{9,11},{10,... | collective-permute-start | bytes 1572872 | tf_op jit(solution)/shard_map/ppermute | solution.py:463
  90.9 26.9 %collective-permute-start.19 = (f32[16,128,128]{2,1,0:T(8,128)S(1)}, f32[16,128,128]{2,1,0:T(8,128)S(1)}, u32[]{:S(2)}, u32[]{:S(2)}) collective-permute-start(f32[16,128,128]{2,1,0:T(8,128)S(1)} %collective-permute-done.17.refs_4_.refs_0_), channel_id=1, source_target_pairs={{0,1},{1,0},{2,3},{3,2},{4,5},{5,4},{6,7},{7,6},{8,9},{9,8},{10,11... | collective-permute-start | bytes 3145736 | tf_op jit(solution)/shard_map/ppermute | solution.py:466
  92.6 21.8 %collective-permute-start.9 = (f32[256,768]{1,0:T(8,128)}, f32[256,768]{1,0:T(8,128)S(1)}, u32[]{:S(2)}, u32[]{:S(2)}) collective-permute-start(f32[256,768]{1,0:T(8,128)} %add.137.refs_0_), channel_id=1, source_target_pairs={{16,0},{24,8},{17,1},{25,9},{26,10},{18,2},{27,11},{19,3},{4,20},{... | collective-permute-start | bytes 2359304 | tf_op jit(solution)/shard_map/ppermute | solution.py:487
  96.2 33.0 %collective-permute-start.15 = (f32[256,768]{1,0:T(8,128)}, f32[256,768]{1,0:T(8,128)S(1)}, u32[]{:S(2)}, u32[]{:S(2)}) collective-permute-start(f32[256,768]{1,0:T(8,128)} %add.138.refs_5_.refs_2_.refs_3_), channel_id=1, source_target_pairs={{8,24},{0,16},{9,25},{1,17},{18,2},{26,10},{19,3},{27,11},{28,12},... | collective-permute-start | bytes 2359304 | tf_op jit(solution)/shard_map/ppermute | solution.py:487
  103.9 13.9 %collective-permute-start.18 = (f32[8,128,128]{2,1,0:T(8,128)S(1)}, f32[8,128,128]{2,1,0:T(8,128)S(1)}, u32[]{:S(2)}, u32[]{:S(2)}) collective-permute-start(f32[8,128,128]{2,1,0:T(8,128)S(1)} %collective-permute-done.16.refs_2_), channel_id=1, source_target_pairs={{0,2},{1,3},{2,4},{3,5},{4,6},{5,7},{6,0},{7,1},{8,10},{9,11},{10,... | collective-permute-start | bytes 1572872 | tf_op jit(solution)/shard_map/ppermute | solution.py:463
  106.3 28.8 %copy-start.19 = (f32[24,128,128]{2,1,0:T(8,128)S(1)}, f32[24,128,128]{2,1,0:T(8,128)}, u32[]{:S(2)}) copy-start(f32[24,128,128]{2,1,0:T(8,128)} %get-tuple-element.228.refs_3_) | copy-start | bytes 4718596
  129.3 2.5 %collective-permute-start.20 = (f32[256,768]{1,0:T(8,128)}, f32[256,768]{1,0:T(8,128)S(1)}, u32[]{:S(2)}, u32[]{:S(2)}) collective-permute-start(f32[256,768]{1,0:T(8,128)} %get-tuple-element.227), channel_id=1, source_target_pairs={{0,8},{8,0},{16,24},{24,16},{1,9},{9,1},{17,25},{25,17},{2,10},{10... | collective-permute-start | bytes 2359304 | tf_op jit(solution)/shard_map/ppermute | solution.py:469
  133.8 21.7 %collective-permute-start.21 = (f32[256,768]{1,0:T(8,128)}, f32[256,768]{1,0:T(8,128)S(1)}, u32[]{:S(2)}, u32[]{:S(2)}) collective-permute-start(f32[256,768]{1,0:T(8,128)} %add.139.refs_4_.refs_6_), channel_id=1, source_target_pairs={{0,16},{8,24},{1,17},{9,25},{10,26},{2,18},{11,27},{3,19},{20,4},{... | collective-permute-start | bytes 2359304 | tf_op jit(solution)/shard_map/ppermute | solution.py:487
  144.4 11.4 %collective-permute-start.23 = (f32[256,768]{1,0:T(8,128)}, f32[256,768]{1,0:T(8,128)S(1)}, u32[]{:S(2)}, u32[]{:S(2)}) collective-permute-start(f32[256,768]{1,0:T(8,128)} %get-tuple-element.230), channel_id=1, source_target_pairs={{0,8},{8,0},{16,24},{24,16},{1,9},{9,1},{17,25},{25,17},{2,10},{10... | collective-permute-start | bytes 2359304 | tf_op jit(solution)/shard_map/ppermute | solution.py:469
  155.7 4.9 %collective-permute-start.22 = (f32[256,768]{1,0:T(8,128)S(1)}, f32[256,768]{1,0:T(8,128)S(1)}, u32[]{:S(2)}, u32[]{:S(2)}) collective-permute-start(f32[256,768]{1,0:T(8,128)S(1)} %pass.1), channel_id=1, source_target_pairs={{0,8},{8,0},{16,24},{24,16},{1,9},{9,1},{17,25},{25,17},{2,10},{10... | collective-permute-start | bytes 2359304 | tf_op jit(solution)/shard_map/ppermute | solution.py:469
  156.8 21.8 %collective-permute-start.24 = (f32[256,768]{1,0:T(8,128)}, f32[256,768]{1,0:T(8,128)S(1)}, u32[]{:S(2)}, u32[]{:S(2)}) collective-permute-start(f32[256,768]{1,0:T(8,128)} %add.140.refs_9_), channel_id=1, source_target_pairs={{24,8},{25,9},{2,18},{3,19},{12,28},{13,29},{22,6},{23,7}} | collective-permute-start | bytes 2359304 | tf_op jit(solution)/shard_map/ppermute | solution.py:478
  158.1 21.2 %collective-permute-start.25 = (f32[256,768]{1,0:T(8,128)}, f32[256,768]{1,0:T(8,128)S(1)}, u32[]{:S(2)}, u32[]{:S(2)}) collective-permute-start(f32[256,768]{1,0:T(8,128)} %add.140.refs_9_), channel_id=1, source_target_pairs={{16,8},{17,9},{10,18},{11,19},{4,28},{5,29},{30,6},{31,7}} | collective-permute-start | bytes 2359304 | tf_op jit(solution)/shard_map/ppermute | solution.py:478
  159.4 19.9 %collective-permute-start.26 = (f32[256,768]{1,0:T(8,128)}, f32[256,768]{1,0:T(8,128)S(1)}, u32[]{:S(2)}, u32[]{:S(2)}) collective-permute-start(f32[256,768]{1,0:T(8,128)} %add.140.refs_9_), channel_id=1, source_target_pairs={{0,8},{1,9},{26,18},{27,19},{20,28},{21,29},{14,6},{15,7}} | collective-permute-start | bytes 2359304 | tf_op jit(solution)/shard_map/ppermute | solution.py:478
  (19 other events, 204.0 us)
